TPU v7x, 32 devices: a whole 2x2x4 slice. The times are simulated.
32 devices in a mesh: row: 4 (over y, x), col: 8 (over z, core).
Axes of the slice: x: 2, y: 2, z: 4, core: 2. Of those that a mesh axis runs over, the one named last changes fastest.
Arguments:
- observed: int32 [8, 768, 2048], P('col', 'row'), may hold values from 0 to 1, as said below
- user_effect: float32 [8, 768], P('col', 'row'), may hold values from -4 to 4
- item_effect: float32 [128, 128], replicated, may hold values from -4 to 4
- block_list: int32 [8, 16], replicated, may hold values from 0 to 127, as said below
Outputs:
- factored: float32 [32, 4, 128, 16, 8, 128], P(None, 'row', None, None, 'col')
- correction: bfloat16 [32, 4, 128, 16, 8, 128], P(None, 'row', None, None, 'col')
- logdet: float32 [], replicated
- pivots: float32 [4, 8, 512], P('row', 'col')
Inputs may be any that keep to these rules, and one draw needn't show every extreme that they name: `block_list`: each row lists 16 distinct tiles; entry k has remainder k // (16 // 4) modulo 4; at most max(1, 16 // 8) entries of a row share a remainder modulo 8, and some remainder reaches that count in every row. `observed`: 1 marks a rating of the user for the item.
All inputs are finite; a program needn't handle non-finite values.
Results may differ from a plain program's by a relative error of at most 0.0069.
Values may be sent and summed in bfloat16 or wider, within the bound.
A program may use at most 320 MiB of HBM per device.

v0:
```python
import jax
import jax.numpy as jnp
from jax import lax
from jax.sharding import PartitionSpec as P

PANEL_BLOCKS = 2


highest = lax.Precision.HIGHEST
user_prior = 1.0
item_prior = 1.0


def broadcast(block, axis, source):
    block = jnp.where(lax.axis_index(axis) == source, block, jnp.zeros_like(block))
    return lax.psum(block, axis)


def body(observed, user_effect, item_effect, block_list):
    rows_n = lax.axis_size("row")
    cols_n = lax.axis_size("col")
    row_idx = lax.axis_index("row")
    col_idx = lax.axis_index("col")
    nblocks, tile = item_effect.shape
    kcount = block_list.shape[1]
    per_row = kcount // rows_n
    slots = max(1, kcount // cols_n)
    width = kcount * tile
    group = per_row * tile
    nb_r = nblocks // rows_n
    nb_c = nblocks // cols_n
    mine = lax.dynamic_index_in_dim(block_list, col_idx, 0, keepdims=False)
    picker = (mine[:, None] == jnp.arange(nblocks)[None, :]).astype(jnp.float32)
    item_vals = jnp.dot(picker, item_effect, precision=highest).reshape(width)
    marks = observed[0]
    prob = jax.nn.sigmoid(user_effect[0][:, None] + item_vals[None, :])
    weight = jnp.where(marks > 0, prob * (1.0 - prob), 0.0)
    precision_u = user_prior + jnp.sum(weight, axis=1)
    scaled = (weight / jnp.sqrt(precision_u)[:, None]).astype(jnp.bfloat16)
    users = scaled.shape[0]
    col_share = lax.psum_scatter(jnp.sum(weight, axis=0), "row", scatter_dimension=0, tiled=True)
    piece = lax.all_gather(scaled, "row", axis=0, tiled=True)
    count = piece.shape[0] // users
    stacked = piece.reshape(count, users, width)
    left = lax.dynamic_slice_in_dim(stacked, row_idx * group, group, 2)
    terms = jnp.einsum("nuk,num->nkm", left, stacked, preferred_element_type=jnp.float32)
    rounded = lax.optimization_barrier(terms.astype(jnp.bfloat16))
    cross = jnp.sum(rounded, axis=0, dtype=jnp.float32)
    global_rows = row_idx * group + jnp.arange(group)
    diag_part = jnp.where(
        global_rows[:, None] == jnp.arange(width)[None, :], col_share[:, None], 0.0
    )
    strip = (diag_part - cross).reshape(per_row, tile, kcount, tile)
    residue = block_list % cols_n
    same = residue[:, :, None] == residue[:, None, :]
    before = jnp.arange(kcount)[None, :] < jnp.arange(kcount)[:, None]
    rank = jnp.sum((same & before[None]).astype(jnp.int32), axis=2)
    my_res = lax.dynamic_index_in_dim(residue, col_idx, 0, keepdims=False)
    my_rank = lax.dynamic_index_in_dim(rank, col_idx, 0, keepdims=False)
    chooser = (
        (my_res[None, None, :] == jnp.arange(cols_n)[:, None, None])
        & (my_rank[None, None, :] == jnp.arange(slots)[None, :, None])
    ).astype(jnp.float32)
    outgoing = jnp.einsum("csk,jakb->csjab", chooser, strip, precision=highest)
    incoming = lax.all_to_all(outgoing, "col", split_axis=0, concat_axis=0, tiled=True)
    picks = (residue == col_idx)[:, None, :] & (
        rank[:, None, :] == jnp.arange(slots)[None, :, None]
    )
    col_block = jnp.sum(jnp.where(picks, block_list[:, None, :], 0), axis=2)
    valid = jnp.any(picks, axis=2)
    row_block = lax.dynamic_slice_in_dim(block_list, row_idx * per_row, per_row, 1)
    local = row_block[:, None, :] // rows_n * nb_c + col_block[:, :, None] // cols_n
    local = jnp.where(valid[:, :, None], local, -1)
    placer = (jnp.arange(nb_r * nb_c)[:, None] == local.reshape(1, -1)).astype(jnp.float32)
    tiles = jnp.dot(placer, incoming.reshape(-1, tile * tile), precision=highest)
    row_ids = jnp.arange(nb_r) * rows_n + row_idx
    col_ids = jnp.arange(nb_c) * cols_n + col_idx
    on_diag = (row_ids[:, None] == col_ids[None, :])[:, :, None, None]
    schur = tiles.reshape(nb_r, nb_c, tile, tile) + jnp.where(
        on_diag, item_prior * jnp.eye(tile, dtype=jnp.float32)[None, None], 0.0
    )
    width_p = PANEL_BLOCKS * tile
    first_col = schur[:, 0]
    slot_mask = (jnp.arange(PANEL_BLOCKS) == col_idx).astype(jnp.float32)
    placed = first_col[:, :, None, :] * slot_mask[None, None, :, None]
    panel = lax.psum(placed, "col").reshape(nb_r, tile, width_p)
    row_mask = (jnp.arange(PANEL_BLOCKS) == row_idx).astype(jnp.float32)
    corner = lax.psum(panel[0][None] * row_mask[:, None, None], "row").reshape(width_p, width_p)
    lower = jnp.linalg.cholesky(corner)
    logdet = 2.0 * jnp.sum(jnp.log(jnp.diagonal(lower)))
    factor_rows = lax.linalg.triangular_solve(
        lower, panel.reshape(nb_r * tile, width_p), left_side=False, lower=True, transpose_a=True
    ).reshape(nb_r, tile, width_p)
    ratio = cols_n // rows_n
    strided = factor_rows.reshape(nb_c, ratio, tile, width_p)
    chosen = lax.dynamic_index_in_dim(strided, col_idx // rows_n, 1, keepdims=False)
    factor_cols = broadcast(chosen, "row", col_idx % rows_n)
    update = jnp.einsum("isk,jtk->ijst", factor_rows, factor_cols, precision=highest)
    own_panel = lax.dynamic_slice_in_dim(
        factor_rows, jnp.minimum(col_idx, PANEL_BLOCKS - 1) * tile, tile, 2
    )
    in_panel = col_ids < PANEL_BLOCKS
    above = row_ids < PANEL_BLOCKS
    trailing = jnp.where(above[:, None, None, None], 0.0, schur - update)
    result = jnp.where(in_panel[None, :, None, None], own_panel[:, None], trailing)
    tile_diag = jnp.diagonal(result, axis1=2, axis2=3)
    diag_vals = jnp.sum(jnp.where(on_diag[:, :, :, 0], tile_diag, 0.0), axis=0)
    pivot_part = lax.psum_scatter(
        diag_vals.reshape(nb_c * tile), "row", scatter_dimension=0, tiled=True
    )
    pivots = pivot_part.reshape(1, 1, pivot_part.shape[0])
    diag_entry = on_diag & jnp.eye(tile, dtype=bool)[None, None]
    cleared = jnp.where(diag_entry, 0.0, result)
    factored = cleared.transpose(0, 2, 1, 3)[:, None, :, :, None, :]
    trailing_mask = (
        jnp.logical_not(above)[:, None, None, None] & jnp.logical_not(in_panel)[None, :, None, None]
    )
    rounded_update = jnp.where(trailing_mask, update, 0.0).astype(jnp.bfloat16)
    corrected = rounded_update.transpose(0, 2, 1, 3)[:, None, :, :, None, :]
    return (factored, corrected, logdet, pivots)


def solution(mesh):
    in_specs = (P("col", "row", None), P("col", "row"), P(), P())
    out_specs = (
        P(None, "row", None, None, "col", None),
        P(None, "row", None, None, "col", None),
        P(),
        P("row", "col", None),
    )
    return jax.shard_map(body, mesh=mesh, in_specs=in_specs, out_specs=out_specs, check_vma=False)
```

profile of v0, /device:TPU:0, one launch (start us, length us, event | category | flops | bytes accessed | tf_op | source)
XLA Modules:
  0.0 772.2 jit_solution(3878546181589672654)
XLA Ops:
  8.2 2.2 fusion.54
  10.4 1.1 divide_convert_fusion
  12.8 11.5 %all-reduce.1 = f32[2048]{0:T(1024)S(1)} all-reduce(f32[2048]{0:T(1024)S(1)} %get-tuple-element.28), channel_id=2, replica_groups=mesh['row'=4,'col'=8] {'row'}, use_global_device_ids=true, to_apply=%region_4.5.clone | all-reduce | flops 2048 | bytes 16384
  24.7 33.6 %all-gather.2.cloned.1.call-done = bf16[768,2048]{1,0:T(8,128)(2,1)} async-done(((bf16[192,2048]{1,0:T(8,128)(2,1)}), bf16[768,2048]{1,0:T(8,128)(2,1)}) %all-gather.2.cloned.1.call-update) | async-done | bytes 3145744 | tf_op jit(solution)/shard_map/all_gather | solution.py:42
  58.3 4.5 convolution_convert_fusion
  62.9 1.9 convert_reduce_fusion
  65.7 2.5 fusion.8
  68.2 2.8 copy.47
  71.0 4.6 all-to-all-start
  76.8 92.9 %all-to-all-done = f32[8,2,4,128,128]{4,3,2,1,0:T(8,128)} async-done(((f32[8,2,4,128,128]{4,3,2,1,0:T(8,128)}), f32[8,2,4,128,128]{4,3,2,1,0:T(8,128)}, u32[]{:S(2)}, u32[]{:S(2)}) %all-to-all-start) | async-done | bytes 4194336 | tf_op jit(solution)/shard_map/all_to_all | solution.py:65
  169.7 35.0 %select_add_fusion = (f32[32,16,128,128]{3,1,2,0:T(8,128)}, f32[32,16,128,128]{3,1,2,0:T(8,128)}) fusion(f32[128,128]{1,0:T(8,128)S(1)} %fusion.35, pred[32,16]{1,0:T(8,128)(4,1)S(1)} %broadcast_compare_fusion, s32[64]{0:T(128)S(1)} %select_n.140, s32[32,16]{1,0:T(8,128)S(1)} %multiply_add_fusion, f32[8,8,128,128]{3,2,1,0:T(8,128)} %bitcast.55), kind=kOutput, calls=%fused_computation.14 | convolution fusion | flops 6459260928 | bytes 71371520 | tf_op jit(solution)/shard_map/dot_general | solution.py:75
  204.7 8.4 %slice.66 = f32[32,1,128,128]{3,1,2,0:T(1,128)} slice(f32[32,16,128,128]{3,1,2,0:T(8,128)} %get-tuple-element.47), slice={[0:32], [0:1], [0:128], [0:128]} | slice | bytes 4194304 | tf_op jit(solution)/shard_map/slice | solution.py:83
  213.1 2.4 copy.49
  215.5 2.7 broadcast_multiply_fusion
  218.3 94.5 %all-reduce.7.cloned.1.call-done = f32[32,128,2,128]{1,0,3,2:T(8,128)} async-done(((f32[32,128,2,128]{1,0,3,2:T(8,128)}), f32[32,128,2,128]{1,0,3,2:T(8,128)}) %all-reduce.7.cloned.1.call-update) | async-done | bytes 4194320 | tf_op jit(solution)/shard_map/psum | solution.py:86
  312.8 1.3 slice.67
  315.1 6.0 copy.84
  321.1 2.0 copy-done.2
  323.1 1.5 triangular_solve.73
  324.6 2.3 copy.66
  326.9 31.8 %all-reduce.9.cloned.1.call-done = f32[256,256]{0,1:T(8,128)} async-done(((f32[256,256]{0,1:T(8,128)}), f32[256,256]{0,1:T(8,128)}) %all-reduce.9.cloned.1.call-update) | async-done | bytes 262160 | tf_op jit(solution)/shard_map/psum | solution.py:88
  360.8 11.7 %cholesky.40 = f32[128,128]{1,0:T(8,128)S(1)} custom-call(f32[128,128]{1,0:T(8,128)S(1)} %cholesky.100), custom_call_target="Cholesky" | custom-call | tf_op jit(solution)/shard_map/jit(cholesky)/cholesky | solution.py:89
  373.2 9.8 %custom-call.14 = f32[1,128,128]{1,2,0:T(8,128)S(1)} custom-call(f32[1,128,128]{2,1,0:T(8,128)S(1)} %get-tuple-element.46), custom_call_target="InvertDiagBlocksLowerTriangular" | custom-call | tf_op jit(solution)/shard_map/jit(cholesky)/cholesky | solution.py:89
  383.6 11.7 %cholesky.87 = f32[128,128]{1,0:T(8,128)S(1)} custom-call(f32[128,128]{1,0:T(8,128)S(1)} %convolution_subtract_fusion.1), custom_call_target="Cholesky" | custom-call | tf_op jit(solution)/shard_map/jit(cholesky)/cholesky | solution.py:89
  397.5 4.1 while.1
  398.1 1.4 bitcast_dynamic-update-slice_fusion.2
  400.1 1.4 bitcast_dynamic-update-slice_fusion.2
  401.6 19.8 %custom-call.15 = f32[2,128,128]{1,2,0:T(8,128)S(1)} custom-call(f32[2,128,128]{2,1,0:T(8,128)S(1)} %get-tuple-element.11), custom_call_target="InvertDiagBlocksLowerTriangular" | custom-call | tf_op jit(solution)/shard_map/triangular_solve | solution.py:91
  421.4 3.6 fusion.14
  425.0 3.5 convolution_subtract_fusion
  428.5 2.0 fusion.30
  430.6 2.5 pad_maximum_fusion
  433.0 6.8 reshape_reshape.7
  439.8 4.4 constant_dynamic-slice_fusion.1
  444.2 4.0 copy.67
  448.2 3.1 select_bitcast_fusion
  451.6 5.6 copy.65
  457.2 2.3 gather_fusion
  460.8 1.7 constant_dynamic-slice_fusion.2
  462.5 58.5 %all-reduce.11.cloned.1.call-done = f32[16,128,256]{2,1,0:T(8,128)} async-done(((f32[16,128,256]{2,1,0:T(8,128)}), f32[16,128,256]{2,1,0:T(8,128)}) %all-reduce.11.cloned.1.call-update) | async-done | bytes 2097168 | tf_op jit(solution)/shard_map/psum | solution.py:16
  521.0 32.7 %fusion.16 = f32[16,128,32,128]{3,1,2,0:T(8,128)} fusion(f32[32,128,256,1]{2,1,0,3:T(8,128)} %bitcast.160, f32[16,128,256]{2,1,0:T(8,128)} %all-reduce.11.cloned.1.call-done), kind=kOutput, calls=%fused_computation.33 | convolution fusion | flops 25769803776 | bytes 39845888 | tf_op jit(solution)/shard_map/isk,jtk->ijst/dot_general | solution.py:98
  553.7 33.4 %copy.55 = f32[16,128,32,128]{1,0,3,2:T(8,128)} copy(f32[16,128,32,128]{3,1,2,0:T(8,128)} %fusion.16) | data formatting | bytes 67108864 | tf_op jit(solution)/shard_map/isk,jtk->ijst/dot_general | solution.py:98
  587.1 17.9 %fusion.6 = bf16[32,1,128,16,1,128]{5,3,4,2,1,0:T(8,128)(2,1)} fusion(f32[16,128,32,128]{1,0,3,2:T(8,128)} %copy.55, pred[32,16]{1,0:T(8,128)(4,1)S(1)} %broadcast_and_fusion), kind=kLoop, calls=%fused_computation.15 | loop fusion | flops 8388608 | bytes 50332160
  605.0 33.6 %fusion.1 = f32[32,16,128,128]{3,1,2,0:T(8,128)} fusion(f32[32,16,128,128]{3,1,2,0:T(8,128)} %get-tuple-element.47, f32[16,128,32,128]{1,0,3,2:T(8,128)} %copy.55, f32[32,128,128]{2,1,0:T(8,128)S(1)} %constant_dynamic-slice_fusion.2, pred[32]{0:T(512)(128)(4,1)S(1)} %get-tuple-element.53, pred[16]{0:T(512)(128)(4,1)S(1)} %get-tuple-element.51), kind=kLoop, calls=%fused_computation.6 | loop fusion | flops 25165824 | bytes 102760496 | tf_op jit(solution)/shard_map/jit(_where)/select_n | solution.py:105
  638.7 80.7 %copy.58 = f32[32,16,128,128]{0,1,3,2:T(8,128)} copy(f32[32,16,128,128]{3,1,2,0:T(8,128)} %fusion.1) | data formatting | bytes 67108864 | tf_op jit(solution)/shard_map/jit(_where)/select_n | solution.py:105
  719.3 2.0 gather_fusion.1
  721.7 9.1 %all-reduce.2 = f32[2048]{0:T(1024)S(1)} all-reduce(f32[2048]{0:T(1024)S(1)} %bitcast.173), channel_id=3, replica_groups=mesh['row'=4,'col'=8] {'row'}, use_global_device_ids=true, to_apply=%region_16.17.clone | all-reduce | flops 2048 | bytes 16384
  731.4 32.7 %fusion.4 = f32[32,128,16,128]{3,2,1,0:T(8,128)} fusion(f32[16,128,32,128]{1,0,3,2:T(8,128)} %copy.55, f32[32,16,128,128]{3,1,2,0:T(8,128)} %get-tuple-element.48, f32[128,128]{1,0:T(8,128)S(1)} %fusion.35, f32[32,128,128]{2,1,0:T(8,128)S(1)} %constant_dynamic-slice_fusion.2, pred[32]{0:T(512)(128)(4,1)S(1)} %get-tuple-element.53, ...), kind=kLoop, calls=%fused_computation.11 | loop fusion | flops 58720256 | bytes 102842928 | tf_op jit(solution)/shard_map/jit(_where)/select_n | solution.py:113
  (78 shorter events, 12.2 us)
Async XLA Ops:
  7.2 0.8 copy-start
  7.2 4.3 copy-start.4
  7.2 17.1 %copy-start.3 = (s32[8,16]{1,0:T(8,128)S(1)}, s32[8,16]{1,0:T(8,128)}, u32[]{:S(2)}) copy-start(s32[8,16]{1,0:T(8,128)} %param.7) | copy-start | bytes 1540
  7.2 51.1 %all-gather.2.cloned.1.call-start = ((), (), s32[]{:S(2)}) async-start(), calls=%async_computation.1 | async-start | bytes 3932160 | tf_op jit(solution)/shard_map/all_gather | solution.py:42
  71.0 98.7 %all-to-all-start = ((f32[8,2,4,128,128]{4,3,2,1,0:T(8,128)}), f32[8,2,4,128,128]{4,3,2,1,0:T(8,128)}, u32[]{:S(2)}, u32[]{:S(2)}) async-start(f32[8,2,4,128,128]{4,3,2,1,0:T(8,128)} %copy.47), calls=%async_computation | async-start | bytes 8388608 | tf_op jit(solution)/shard_map/all_to_all | solution.py:65
  75.6 237.2 %all-reduce.7.cloned.1.call-start = ((), (), s32[]{:S(2)}) async-start(), calls=%async_computation.2 | async-start | bytes 8388608 | tf_op jit(solution)/shard_map/psum | solution.py:86
  218.2 140.6 %all-reduce.9.cloned.1.call-start = ((), (), s32[]{:S(2)}) async-start(), calls=%async_computation.3 | async-start | bytes 524288 | tf_op jit(solution)/shard_map/psum | solution.py:88
  315.0 206.0 %all-reduce.11.cloned.1.call-start = ((), (), s32[]{:S(2)}) async-start(), calls=%async_computation.4 | async-start | bytes 4194304 | tf_op jit(solution)/shard_map/psum | solution.py:16
  321.1 2.0 copy-start.2
  731.4 32.7 %copy-start.1 = (f32[128,128]{1,0:T(8,128)S(1)}, f32[128,128]{1,0:T(8,128)}, u32[]{:S(2)}) copy-start(f32[128,128]{1,0:T(8,128)} %param.6) | copy-start | bytes 196612
Sparse Core Ops, SparseCore 0:
  11.6 46.6 all-gather.1
  218.3 94.4 all-reduce.6
  315.7 42.9 all-reduce.8
  451.4 69.5 all-reduce.10
where the time goes:
time: 783 us; the launch traced here: 772 us
  waiting for transfers between devices  311 us (40%)
  local copies, waits for them, and re-layouts  177 us (23%)
  other arithmetic  155 us (20%)
  matrix products  84.5 us (11%)
  blocking collectives  20.6 us (3%)
  between operations  18.4 us (2%)
    psum x1, waiting for transfers between devices, body(): panel = lax.psum(placed, 'col').reshape(nb_r, tile, width_p)  94.5 us
    all_to_all x1, waiting for transfers between devices, body(): lax.all_to_all(outgoing, 'col', split_axis=0, concat_axis=0, tiled=True)  92.9 us
    select_n x1, local copies, waits for them, and re-layouts, body(): jnp.where(in_panel[None, :, None, None], own_panel[:, None], trailing)  80.7 us
    psum x1, waiting for transfers between devices, broadcast(): return lax.psum(block, axis)  58.5 us
    dot_general x1, matrix products, body(): jnp.dot(placer, incoming.reshape(-1, tile * tile), precision=highest)  35 us
    another operation x7, other arithmetic, body(): lower = jnp.linalg.cholesky(corner)  34.7 us
    select_n x1, other arithmetic, body(): jnp.where(in_panel[None, :, None, None], own_panel[:, None], trailing)  33.6 us
    all_gather x1, waiting for transfers between devices, body(): piece = lax.all_gather(scaled, 'row', axis=0, tiled=True)  33.6 us
  transfers between devices with their start and end apart: 5, of which 5 were waited for; matrix products, arithmetic and copies ran while one was open for 3% of the time, Pallas kernels for 0%

commit v1 on v0

v1 whole, which is shorter than its diff:
```python
import functools

import jax
import jax.numpy as jnp
from jax import lax
from jax.experimental import pallas as pl
from jax.experimental.pallas import tpu as pltpu
from jax.sharding import PartitionSpec as P

PANEL_BLOCKS = 2
EXTRA = 16
MESH = pl.DeviceIdType.MESH
HBM = pl.BlockSpec(memory_space=pl.ANY)
VMEM = pl.BlockSpec(memory_space=pltpu.VMEM)
SMEM = pl.BlockSpec(memory_space=pltpu.SMEM)

highest = lax.Precision.HIGHEST
user_prior = 1.0
item_prior = 1.0
BIG = 56 * 1024 * 1024


def dot_nt(a, b, precision=highest):
    return lax.dot_general(
        a, b, (((1,), (1,)), ((), ())), precision=precision, preferred_element_type=jnp.float32
    )


def dot_tn(a, b, precision=None):
    return lax.dot_general(
        a, b, (((0,), (0,)), ((), ())), precision=precision, preferred_element_type=jnp.float32
    )


def weight_kernel(kcount, tile, ids, blocks, observed, effect, items, out, weight):
    users = effect.shape[0]
    col = ids[1]
    user = effect[...]
    total = jnp.zeros((users, tile), jnp.float32)
    for k in range(kcount):
        span = pl.ds(k * tile, tile)
        prob = jax.nn.sigmoid(user + items[pl.ds(blocks[col, k], 1), :])
        part = jnp.where(observed[:, span] > 0, prob * (1.0 - prob), 0.0)
        weight[:, span] = part
        total = total + part
    scale = 1.0 / jnp.sqrt(user_prior + jnp.sum(total, axis=1, keepdims=True))
    line = lax.broadcasted_iota(jnp.int32, (EXTRA, tile), 0)
    for k in range(kcount):
        span = pl.ds(k * tile, tile)
        part = weight[:, span]
        out[pl.ds(0, users), span] = (part * scale).astype(jnp.bfloat16)
        sums = jnp.sum(part, axis=0, keepdims=True)
        high = sums.astype(jnp.bfloat16).astype(jnp.float32)
        mid = (sums - high).astype(jnp.bfloat16).astype(jnp.float32)
        low = sums - high - mid
        rows = jnp.where(line == 0, high, jnp.where(line == 1, mid, jnp.where(line == 2, low, 0.0)))
        out[pl.ds(users, EXTRA), span] = rows.astype(jnp.bfloat16)


def greet(peers):
    barrier = pltpu.get_barrier_semaphore()
    for peer in peers:
        pl.semaphore_signal(barrier, inc=1, device_id=peer, device_id_type=MESH)
    pl.semaphore_wait(barrier, len(peers))


def remote(src, dst, send, recv, peer):
    return pltpu.make_async_remote_copy(
        src_ref=src, dst_ref=dst, send_sem=send, recv_sem=recv, device_id=peer, device_id_type=MESH
    )


def gather_rows_kernel(rows_n, mine, out, sends, recvs, local):
    row = lax.axis_index("row")
    col = lax.axis_index("col")
    if rows_n == 4:
        x = row % 2
        y = row // 2
        px = y * 2 + (1 - x)
        py = (1 - y) * 2 + x
        pd = (1 - y) * 2 + (1 - x)
        greet([(px, col), (py, col)])
        half = mine.shape[0] // 2
        part = [pl.ds(0, half), pl.ds(half, half)]
        jobs = {}
        for n, (axis, h) in enumerate(((0, 0), (1, 1), (0, 1), (1, 0))):
            peer = (px, col) if axis == 0 else (py, col)
            jobs[(axis, h)] = remote(
                mine.at[part[h]], out.at[row, part[h]], sends.at[n], recvs.at[n], peer
            )
            jobs[(axis, h)].start()
        keep = pltpu.make_async_copy(mine, out.at[row], local)
        keep.start()
        jobs[(0, 0)].wait_recv()
        far0 = remote(out.at[px, part[0]], out.at[px, part[0]], sends.at[4], recvs.at[4], (py, col))
        far0.start()
        jobs[(1, 1)].wait_recv()
        far1 = remote(out.at[py, part[1]], out.at[py, part[1]], sends.at[5], recvs.at[5], (px, col))
        far1.start()
        jobs[(0, 1)].wait_recv()
        jobs[(1, 0)].wait_recv()
        far0.wait_recv()
        far1.wait_recv()
        for job in jobs.values():
            job.wait_send()
        far0.wait_send()
        far1.wait_send()
        keep.wait()
    else:
        peers = [(lax.rem(row + k, rows_n), col) for k in range(1, rows_n)]
        greet(peers)
        jobs = []
        for k, peer in enumerate(peers):
            jobs.append(remote(mine, out.at[row], sends.at[k], recvs.at[k], peer))
            jobs[-1].start()
        keep = pltpu.make_async_copy(mine, out.at[row], local)
        keep.start()
        for job in jobs:
            job.wait()
        keep.wait()


def product_kernel(per_row, tile, rows_n, cols_n, slots, ids, blocks, stacked, out, panel, left, count):
    users = stacked.shape[1] - EXTRA
    kcount = blocks.shape[1]
    group = per_row * tile
    row = ids[0]
    col = ids[1]
    left[...] = stacked[:, pl.ds(0, users), pl.ds(pl.multiple_of(row * group, tile), group)]
    panel[...] = jnp.zeros_like(panel)
    for c in range(cols_n):
        count[c] = 0
    eye = lax.broadcasted_iota(jnp.int32, (tile, tile), 0) == lax.broadcasted_iota(
        jnp.int32, (tile, tile), 1
    )

    @pl.loop(0, kcount)
    def _(k):
        block = blocks[col, k]
        span = pl.ds(pl.multiple_of(k * tile, tile), tile)
        cross = jnp.zeros((group, tile), jnp.float32)
        for g in range(rows_n):
            term = dot_tn(left[g], stacked[g, pl.ds(0, users), span])
            cross = cross + term.astype(jnp.bfloat16).astype(jnp.float32)
        total = jnp.zeros((1, tile), jnp.float32)
        for g in range(rows_n):
            extra = stacked[g, pl.ds(users, EXTRA), span].astype(jnp.float32)
            total = total + jnp.sum(extra, axis=0, keepdims=True)
        residue = lax.rem(block, cols_n)
        slot = count[residue]
        count[residue] = slot + 1
        place = residue * slots + jnp.minimum(slot, slots - 1)
        for j in range(per_row):
            part = -cross[j * tile : (j + 1) * tile]
            part = part + jnp.where(eye & (row * per_row + j == k), total, 0.0)
            part = part.astype(jnp.bfloat16)
            out[place, pl.ds(j * tile, tile), :] = part
            for b in range(PANEL_BLOCKS):

                @pl.when(block == b)
                def _():
                    panel[pl.ds(j * tile, tile), pl.ds(b * tile, tile)] = part


def gather_cols_kernel(cols_n, mine, out, sends, recvs, local):
    row = lax.axis_index("row")
    col = lax.axis_index("col")
    core = col % 2
    place = col // 2
    deep = cols_n // 2
    mate = (row, place * 2 + 1 - core)
    others = [lax.rem(place + k, deep) * 2 + core for k in range(1, deep)]
    greet([mate] + [(row, c) for c in others])
    jobs = []
    for k, c in enumerate(others):
        jobs.append(remote(mine, out.at[col], sends.at[k], recvs.at[k], (row, c)))
        jobs[-1].start()
    share = [remote(mine, out.at[col], sends.at[deep], recvs.at[deep], mate)]
    share[0].start()
    keep = pltpu.make_async_copy(mine, out.at[col], local)
    keep.start()
    for k in range(1, deep):
        source = lax.rem(place - k + deep, deep) * 2 + core
        jobs[k - 1].wait_recv()
        share.append(
            remote(out.at[source], out.at[source], sends.at[deep + k], recvs.at[deep + k], mate)
        )
        share[-1].start()
    for job in share:
        job.wait_recv()
    for job in jobs + share:
        job.wait_send()
    keep.wait()


def dense_kernel(per_row, tile, rows_n, ids, blocks, gathered, dense, corner, work):
    nb_r = dense.shape[0]
    cols_n = blocks.shape[0]
    row = ids[0]
    work[...] = jnp.zeros_like(work)
    shape = (tile, work.shape[2])
    first = lax.broadcasted_iota(jnp.int32, shape, 0)
    second = lax.broadcasted_iota(jnp.int32, shape, 1)
    unit = jnp.where((first + row * tile == second) & (row < PANEL_BLOCKS), item_prior, 0.0)
    work[0] = unit.astype(jnp.float32)

    @pl.loop(0, cols_n)
    def _(c):
        for j in range(per_row):
            place = blocks[c, row * per_row + j] // rows_n
            work[place] = work[place] + gathered[c, pl.ds(j * tile, tile), :].astype(jnp.float32)

    corner[...] = work[0]
    dense[...] = work[...].astype(jnp.bfloat16)


def share_rows_kernel(rows_n, dense, corner, cols, corners, sends, recvs, csends, crecvs, local):
    row = lax.axis_index("row")
    col = lax.axis_index("col")
    ratio_part = col // rows_n
    owner = lax.rem(col, rows_n)
    peers = [(lax.rem(row + k, rows_n), col) for k in range(1, rows_n)]
    greet(peers)
    for b in range(PANEL_BLOCKS):

        @pl.when(row == b)
        def _():
            for k, peer in enumerate(peers):
                remote(corner, corners.at[b], csends.at[k], crecvs.at[b], peer).start()
            pltpu.make_async_copy(corner, corners.at[b], local.at[0]).start()

    @pl.when(row == owner)
    def _():
        for k, peer in enumerate(peers):
            remote(dense.at[:, ratio_part], cols, sends.at[k], recvs.at[0], peer).start()
        pltpu.make_async_copy(dense.at[:, ratio_part], cols, local.at[1]).start()

    for b in range(PANEL_BLOCKS):

        @pl.when(row == b)
        def _():
            for k, peer in enumerate(peers):
                remote(corner, corners.at[b], csends.at[k], crecvs.at[b], peer).wait_send()
            pltpu.make_async_copy(corner, corners.at[b], local.at[0]).wait()

        @pl.when(row != b)
        def _():
            remote(corner, corners.at[b], csends.at[0], crecvs.at[b], peers[0]).wait_recv()

    @pl.when(row == owner)
    def _():
        for k, peer in enumerate(peers):
            remote(dense.at[:, ratio_part], cols, sends.at[k], recvs.at[0], peer).wait_send()
        pltpu.make_async_copy(dense.at[:, ratio_part], cols, local.at[1]).wait()

    @pl.when(row != owner)
    def _():
        remote(dense.at[:, ratio_part], cols, sends.at[0], recvs.at[0], peers[0]).wait_recv()


def eliminate(work, tile):
    first = lax.broadcasted_iota(jnp.int32, (tile, tile), 0)
    second = lax.broadcasted_iota(jnp.int32, (tile, tile), 1)
    lane = lax.broadcasted_iota(jnp.int32, (1, tile), 1)
    sub = lax.broadcasted_iota(jnp.int32, (tile, 1), 0)

    @pl.loop(0, tile)
    def _(j):
        now = work[...]
        line = work[pl.ds(j, 1), :]
        pivot = jnp.sum(jnp.where(lane == j, line, 0.0), axis=1, keepdims=True)
        column = jnp.sum(jnp.where(second == j, now, 0.0), axis=1, keepdims=True)
        factor = jnp.where(sub > j, column / pivot, 0.0)
        base = jnp.where((second == j) & (first > j), 0.0, now)
        work[...] = base - factor * jnp.where(lane == j, 1.0, line)

    done = work[...]
    eye = first == second
    pivot_col = jnp.sum(jnp.where(eye, done, 0.0), axis=1, keepdims=True)
    unit = jnp.where(eye, 1.0, jnp.where(first > second, done, 0.0))
    return unit / jnp.sqrt(pivot_col), jnp.sum(jnp.log(pivot_col), axis=0, keepdims=True)


def solve_kernel(tile, corners, dense, cols, rows_out, cols_out, exact, logdet, work, inverse):
    nb_r = dense.shape[0]
    a11 = corners[0, :, pl.ds(0, tile)]
    work[...] = a11
    w1, log1 = eliminate(work, tile)
    a21 = corners[1, :, pl.ds(0, tile)]
    l21 = dot_nt(a21, w1)
    work[...] = corners[1, :, pl.ds(tile, tile)] - dot_nt(l21, l21)
    w2, log2 = eliminate(work, tile)
    cross = jnp.dot(l21, w1, precision=highest, preferred_element_type=jnp.float32)
    w21 = -jnp.dot(w2, cross, precision=highest, preferred_element_type=jnp.float32)
    inverse[pl.ds(0, tile), pl.ds(0, tile)] = w1
    inverse[pl.ds(0, tile), pl.ds(tile, tile)] = jnp.zeros((tile, tile), jnp.float32)
    inverse[pl.ds(tile, tile), pl.ds(0, tile)] = w21
    inverse[pl.ds(tile, tile), pl.ds(tile, tile)] = w2
    logdet[...] = jnp.broadcast_to(log1 + log2, logdet.shape)
    full = inverse[...]
    high = full.astype(jnp.bfloat16)
    low = (full - high.astype(jnp.float32)).astype(jnp.bfloat16)

    def apply(block):
        return dot_nt(block, high, None) + dot_nt(block, low, None)

    @pl.loop(0, nb_r)
    def _(i):
        got = apply(dense[i])
        rows_out[i] = got.astype(jnp.bfloat16)
        exact[i] = got

    @pl.loop(0, cols.shape[0])
    def _(i):
        cols_out[i] = apply(cols[i]).astype(jnp.bfloat16)


def final_kernel(
    per_row, slots, rows_n, cols_n, ids, blocks, rows_ref, cols_ref, own_ref, tiles,
    full, corr, diag, upd, col_tab, row_cnt, row_tab
):
    i = pl.program_id(0)
    nb_r = pl.num_programs(0)
    tile = rows_ref.shape[1]
    nb_c = cols_ref.shape[0]
    kcount = blocks.shape[1]
    row = ids[0]
    col = ids[1]

    @pl.when(i == 0)
    def _():
        diag[...] = jnp.zeros_like(diag)

        @pl.loop(0, nb_r)
        def _(n):
            row_cnt[n] = 0

        @pl.loop(0, cols_n)
        def _(c):
            for s in range(slots):
                col_tab[c * slots + s] = -1

            def scan(k, seen):
                block = blocks[c, k]
                hit = lax.rem(block, cols_n) == col

                @pl.when(hit)
                def _():
                    col_tab[c * slots + jnp.minimum(seen, slots - 1)] = block // cols_n

                return seen + hit.astype(jnp.int32)

            lax.fori_loop(0, kcount, scan, jnp.int32(0))
            shift = lax.rem(col - c + cols_n, cols_n)
            for j in range(per_row):
                place = blocks[c, row * per_row + j] // rows_n
                n = row_cnt[place]
                row_cnt[place] = n + 1
                row_tab[place * cols_n + n] = c * (cols_n * per_row) + shift * per_row + j

    above = i * rows_n + row < PANEL_BLOCKS
    left = rows_ref[0]
    for jj in range(nb_c):
        upd[pl.ds(jj, tile, stride=nb_c), :] = dot_nt(left, cols_ref[jj], None)
    in_panel = col < PANEL_BLOCKS
    place = lax.rem(lax.broadcasted_iota(jnp.int32, (tile * nb_c, upd.shape[1]), 0), nb_c)

    @pl.when(above)
    def _():
        corr[0] = jnp.zeros(corr.shape[1:], corr.dtype)
        full[0] = jnp.zeros(full.shape[1:], full.dtype)

    @pl.when(jnp.logical_not(above))
    def _():
        value = upd[...]
        full[0] = -value
        corr[0] = jnp.where((place == 0) & in_panel, 0.0, value).astype(corr.dtype)

        @pl.loop(0, row_cnt[i])
        def _(n):
            code = row_tab[i * cols_n + n]
            c = code // (cols_n * per_row)
            rest = lax.rem(code, cols_n * per_row)
            shift = rest // per_row
            j = lax.rem(rest, per_row)
            for s in range(slots):
                jj = col_tab[c * slots + s]

                @pl.when(jj >= 0)
                def _():
                    part = tiles[shift, s, pl.ds(pl.multiple_of(j * tile, tile), tile), :]
                    where = pl.ds(jj, tile, stride=nb_c)
                    full[0, where, :] = full[0, where, :] + part.astype(jnp.float32)

    @pl.when(in_panel)
    def _():
        full[0, pl.ds(0, tile, stride=nb_c), :] = own_ref[0]

    far = i * rows_n + row - col

    @pl.when((far >= 0) & (lax.rem(far + cols_n * nb_c, cols_n) == 0))
    def _():
        jj = far // cols_n
        where = pl.ds(jj, tile, stride=nb_c)
        block = full[0, where, :]
        eye = lax.broadcasted_iota(jnp.int32, block.shape, 0) == lax.broadcasted_iota(
            jnp.int32, block.shape, 1
        )
        full[0, where, :] = jnp.where(eye, 0.0, block)
        prior = jnp.where(jnp.logical_or(above, in_panel & (jj == 0)), 0.0, item_prior)
        diag[pl.ds(jj, 1), :] = jnp.sum(jnp.where(eye, block, 0.0), axis=0, keepdims=True) + prior


def params(limit=BIG, **kw):
    return pltpu.CompilerParams(vmem_limit_bytes=limit, **kw)


def body(observed, user_effect, item_effect, block_list):
    rows_n = lax.axis_size("row")
    cols_n = lax.axis_size("col")
    row_idx = lax.axis_index("row")
    col_idx = lax.axis_index("col")
    nblocks, tile = item_effect.shape
    kcount = block_list.shape[1]
    per_row = kcount // rows_n
    slots = max(1, kcount // cols_n)
    width = kcount * tile
    group = per_row * tile
    nb_r = nblocks // rows_n
    nb_c = nblocks // cols_n
    users = observed.shape[1]
    width_p = PANEL_BLOCKS * tile
    ids = jnp.stack([row_idx, col_idx]).astype(jnp.int32)
    f32, bf16 = jnp.float32, jnp.bfloat16
    dma = pltpu.SemaphoreType.DMA

    mine = pl.pallas_call(
        functools.partial(weight_kernel, kcount, tile),
        out_shape=jax.ShapeDtypeStruct((users + EXTRA, width), bf16),
        in_specs=[SMEM, SMEM, VMEM, VMEM, VMEM],
        out_specs=VMEM,
        scratch_shapes=[pltpu.VMEM((users, width), f32)],
        compiler_params=params(),
        name="weights",
    )(ids, block_list, observed[0], user_effect.reshape(users, 1), item_effect)

    stacked = pl.pallas_call(
        functools.partial(gather_rows_kernel, rows_n),
        out_shape=jax.ShapeDtypeStruct((rows_n, users + EXTRA, width), bf16),
        in_specs=[HBM],
        out_specs=HBM,
        scratch_shapes=[dma((max(6, rows_n),)), dma((max(6, rows_n),)), dma],
        compiler_params=params(2**20, collective_id=0, has_side_effects=True),
        name="gather_rows",
    )(mine)

    strips, panel = pl.pallas_call(
        functools.partial(product_kernel, per_row, tile, rows_n, cols_n, slots),
        out_shape=(
            jax.ShapeDtypeStruct((cols_n * slots, group, tile), bf16),
            jax.ShapeDtypeStruct((group, width_p), bf16),
        ),
        in_specs=[SMEM, SMEM, VMEM],
        out_specs=(VMEM, VMEM),
        scratch_shapes=[pltpu.VMEM((rows_n, users, group), bf16), pltpu.SMEM((cols_n,), jnp.int32)],
        compiler_params=params(),
        name="products",
    )(ids, block_list, stacked)

    gathered = pl.pallas_call(
        functools.partial(gather_cols_kernel, cols_n),
        out_shape=jax.ShapeDtypeStruct((cols_n, group, width_p), bf16),
        in_specs=[HBM],
        out_specs=HBM,
        scratch_shapes=[dma((cols_n,)), dma((cols_n,)), dma],
        compiler_params=params(2**20, collective_id=1, has_side_effects=True),
        name="gather_cols",
    )(panel)

    strips = strips.reshape(cols_n, slots, group, tile)
    parts = [lax.dynamic_slice_in_dim(strips, col_idx, 1, 0)]
    for k in range(1, cols_n):
        part = lax.dynamic_slice_in_dim(strips, lax.rem(col_idx + k, cols_n), 1, 0)
        parts.append(lax.ppermute(part, "col", [(c, (c + k) % cols_n) for c in range(cols_n)]))
    tiles = jnp.concatenate(parts, axis=0)

    dense, corner = pl.pallas_call(
        functools.partial(dense_kernel, per_row, tile, rows_n),
        out_shape=(
            jax.ShapeDtypeStruct((nb_r, tile, width_p), bf16),
            jax.ShapeDtypeStruct((tile, width_p), f32),
        ),
        in_specs=[SMEM, SMEM, VMEM],
        out_specs=(VMEM, VMEM),
        scratch_shapes=[pltpu.VMEM((nb_r, tile, width_p), f32)],
        compiler_params=params(),
        name="dense",
    )(ids, block_list, gathered)

    ratio = cols_n // rows_n
    panel_cols, corners = pl.pallas_call(
        functools.partial(share_rows_kernel, rows_n),
        out_shape=(
            jax.ShapeDtypeStruct((nb_c, tile, width_p), bf16),
            jax.ShapeDtypeStruct((PANEL_BLOCKS, tile, width_p), f32),
        ),
        in_specs=[HBM, HBM],
        out_specs=(HBM, HBM),
        scratch_shapes=[
            dma((rows_n,)), dma((1,)), dma((rows_n,)), dma((PANEL_BLOCKS,)), dma((2,)),
        ],
        compiler_params=params(2**20, collective_id=2, has_side_effects=True),
        name="share_rows",
    )(dense.reshape(nb_c, ratio, tile, width_p), corner)

    rows_f, cols_f, exact, logs = pl.pallas_call(
        functools.partial(solve_kernel, tile),
        out_shape=(
            jax.ShapeDtypeStruct((nb_r, tile, width_p), bf16),
            jax.ShapeDtypeStruct((nb_c, tile, width_p), bf16),
            jax.ShapeDtypeStruct((nb_r, tile, width_p), f32),
            jax.ShapeDtypeStruct((8, tile), f32),
        ),
        in_specs=[VMEM, VMEM, VMEM],
        out_specs=(VMEM, VMEM, VMEM, VMEM),
        scratch_shapes=[pltpu.VMEM((tile, tile), f32), pltpu.VMEM((width_p, width_p), f32)],
        compiler_params=params(),
        name="solve",
    )(corners, dense, panel_cols)
    logdet = logs[0, 0]

    rows_all = tile * nb_c
    full, corr, diag = pl.pallas_call(
        functools.partial(final_kernel, per_row, slots, rows_n, cols_n),
        grid_spec=pltpu.PrefetchScalarGridSpec(
            num_scalar_prefetch=2,
            grid=(nb_r,),
            in_specs=[
                pl.BlockSpec((1, tile, width_p), lambda i, ids, bl: (i, 0, 0)),
                pl.BlockSpec((nb_c, tile, width_p), lambda i, ids, bl: (0, 0, 0)),
                pl.BlockSpec(
                    (1, tile, tile), lambda i, ids, bl: (i, 0, jnp.minimum(ids[1], PANEL_BLOCKS - 1))
                ),
                pl.BlockSpec((cols_n, slots, group, tile), lambda i, ids, bl: (0, 0, 0, 0)),
            ],
            out_specs=[
                pl.BlockSpec((1, rows_all, tile), lambda i, ids, bl: (i, 0, 0)),
                pl.BlockSpec((1, rows_all, tile), lambda i, ids, bl: (i, 0, 0)),
                pl.BlockSpec((nb_c, tile), lambda i, ids, bl: (0, 0)),
            ],
            scratch_shapes=[
                pltpu.VMEM((rows_all, tile), f32),
                pltpu.SMEM((cols_n * slots,), jnp.int32),
                pltpu.SMEM((nb_r,), jnp.int32),
                pltpu.SMEM((nb_r * cols_n,), jnp.int32),
            ],
        ),
        out_shape=(
            jax.ShapeDtypeStruct((nb_r, rows_all, tile), f32),
            jax.ShapeDtypeStruct((nb_r, rows_all, tile), bf16),
            jax.ShapeDtypeStruct((nb_c, tile), f32),
        ),
        compiler_params=params(),
        name="final",
    )(ids, block_list, rows_f, cols_f, exact, tiles)

    pivot_part = lax.psum_scatter(diag.reshape(nb_c * tile), "row", scatter_dimension=0, tiled=True)
    pivots = pivot_part.reshape(1, 1, pivot_part.shape[0])
    out = (nb_r, 1, tile, nb_c, 1, tile)
    return (full.reshape(out), corr.reshape(out), logdet, pivots)


def solution(mesh):
    in_specs = (P("col", "row", None), P("col", "row"), P(), P())
    out_specs = (
        P(None, "row", None, None, "col", None),
        P(None, "row", None, None, "col", None),
        P(),
        P("row", "col", None),
    )
    return jax.shard_map(body, mesh=mesh, in_specs=in_specs, out_specs=out_specs, check_vma=False)
```

time: 783 us -> 259 us (0.33); the launches traced: 772 us -> 256 us
  waiting for transfers between devices: 311 us -> 9.04 us
  Pallas kernels: 0 us -> 204 us
  local copies, waits for them, and re-layouts: 177 us -> 21.2 us
  other arithmetic: 155 us -> 0.62 us
  matrix products: 84.5 us -> 0 us
  between operations: 18.4 us -> 1.48 us
  blocking collectives: 20.6 us -> 10.3 us
    pallas_call x0 -> x8, Pallas kernels: none -> 204 us  [the longest x1 42.5 us: body(): pl.pallas_call(functools.partial(gather_cols_kernel, cols_n), out_shape=j...]
    psum x3 -> x0, waiting for transfers between devices: 185 us -> none  [the longest x1 94.5 us: body(): panel = lax.psum(placed, 'col').reshape(nb_r, tile, width_p)]
    all_to_all x1 -> x0, waiting for transfers between devices: 92.9 us -> none  [body(): lax.all_to_all(outgoing, 'col', split_axis=0, concat_axis=0, tiled=True)]
    select_n x3 -> x0, local copies, waits for them, and re-layouts: 80.8 us -> none  [the longest x1 80.7 us: body(): jnp.where(in_panel[None, :, None, None], own_panel[:, None], trailing)]
    dot_general x5 -> x0, matrix products: 74.9 us -> none  [the longest x1 35 us: body(): jnp.dot(placer, incoming.reshape(-1, tile * tile), precision=highest)]
    select_n x6 -> x0, other arithmetic: 69.5 us -> none  [the longest x1 33.6 us: body(): jnp.where(in_panel[None, :, None, None], own_panel[:, None], trailing)]
    another operation x11 -> x1, other arithmetic: 57 us -> 0.62 us  [body(): ids = jnp.stack([row_idx, col_idx]).astype(jnp.int32)]
    dot_general x2 -> x0, local copies, waits for them, and re-layouts: 36.2 us -> none  [the longest x1 33.4 us: body(): jnp.einsum('isk,jtk->ijst', factor_rows, factor_cols, precision=highest)]
  transfers between devices with their start and end apart: 5 -> 7, of which waited for: 5 -> 1; matrix products, arithmetic and copies ran while one was open for 3% -> 2% of each run, Pallas kernels for 0% -> 46%
where the time goes in v1:
time: 259 us; the launch traced here: 256 us
  Pallas kernels  204 us (79%)
  local copies, waits for them, and re-layouts  21.2 us (8%)
  blocking collectives  10.3 us (4%)
  starting transfers between devices  10.2 us (4%)
  waiting for transfers between devices  9.04 us (3%)
    pallas_call x1, Pallas kernels, body(): pl.pallas_call(functools.partial(gather_cols_kernel, cols_n), out_shape=j...  42.5 us
    pallas_call x1, Pallas kernels, body(): pl.pallas_call(functools.partial(solve_kernel, tile), out_shape=(jax.Shap...  42.4 us
    pallas_call x1, Pallas kernels, body(): pl.pallas_call(functools.partial(final_kernel, per_row, slots, rows_n, co...  37 us
    pallas_call x1, Pallas kernels, body(): pl.pallas_call(functools.partial(gather_rows_kernel, rows_n), out_shape=j...  32.4 us
    pallas_call x1, Pallas kernels, body(): pl.pallas_call(functools.partial(share_rows_kernel, rows_n), out_shape=(j...  30.2 us
    unnamed x28, local copies, waits for them, and re-layouts  15 us
    pallas_call x1, Pallas kernels, body(): pl.pallas_call(functools.partial(product_kernel, per_row, tile, rows_n, c...  12.1 us
    unnamed x1, blocking collectives  10.3 us
  transfers between devices with their start and end apart: 7, of which 1 were waited for; matrix products, arithmetic and copies ran while one was open for 2% of the time, Pallas kernels for 46%

profile of v1, /device:TPU:0, one launch (start us, length us, event | category | flops | bytes accessed | tf_op | source)
XLA Modules:
  0.0 256.4 jit_solution(14770862249450442796)
XLA Ops:
  0.7 1.4 copy.13.effect
  2.1 0.6 pad_add_fusion.ids
  2.7 3.1 %weights.1.mine = bf16[208,2048]{1,0:T(8,128)(2,1)} custom-call(s32[2]{0:T(128)} %pad_add_fusion.ids, s32[8,16]{1,0:T(8,128)} %blocks.7, s32[192,2048]{1,0:T(8,128)} %bitcast.18, f32[192,1]{1,0:T(8,128)} %copy.13.effect, f32[128,128]{1,0:T(8,128)} %items.1), custom_call_target="tpu_custom_call" | custom-call | tf_op jit(solution)/shard_map/weights/pallas_call | solution.py:437
  5.8 1.2 copy-done.3
  7.0 32.4 %gather_rows.1.stacked = bf16[4,208,2048]{2,1,0:T(8,128)(2,1)S(1)} custom-call(bf16[208,2048]{1,0:T(8,128)(2,1)S(1)} %copy-done.3), custom_call_target="tpu_custom_call" | custom-call | tf_op jit(solution)/shard_map/gather_rows/pallas_call | solution.py:447
  39.4 0.0 copy-start
  39.4 1.7 copy-done
  41.1 12.1 %products.1 = (bf16[16,512,128]{2,1,0:T(8,128)(2,1)}, bf16[512,256]{1,0:T(8,128)(2,1)}) custom-call(s32[2]{0:T(128)} %pad_add_fusion.ids, s32[8,16]{1,0:T(8,128)} %blocks.7, bf16[4,208,2048]{2,1,0:T(8,128)(2,1)} %copy-done), custom_call_target="tpu_custom_call" | custom-call | tf_op jit(solution)/shard_map/products/pallas_call | solution.py:457
  53.2 2.5 constant_dynamic-slice_fusion
  55.8 0.0 collective-permute-start
  55.8 1.6 collective-permute-start.1
  57.4 2.6 collective-permute-start.2
  59.9 1.1 collective-permute-start.6
  61.0 1.2 collective-permute-start.5
  62.2 0.0 copy-done.5
  62.2 42.5 %gather_cols.1.gathered = bf16[8,512,256]{2,1,0:T(8,128)(2,1)S(1)} custom-call(bf16[512,256]{1,0:T(8,128)(2,1)S(1)} %copy-done.5), custom_call_target="tpu_custom_call" | custom-call | tf_op jit(solution)/shard_map/gather_cols/pallas_call | solution.py:470
  104.7 0.0 copy-start.1
  104.7 1.3 copy-done.1
  106.1 3.9 %dense.1 = (bf16[32,128,256]{2,1,0:T(8,128)(2,1)}, f32[128,256]{1,0:T(8,128)}) custom-call(s32[2]{0:T(128)} %pad_add_fusion.ids, s32[8,16]{1,0:T(8,128)} %blocks.7, bf16[8,512,256]{2,1,0:T(8,128)(2,1)} %copy-done.1), custom_call_target="tpu_custom_call" | custom-call | tf_op jit(solution)/shard_map/dense/pallas_call | solution.py:487
  110.0 1.6 copy-done.2
  111.5 0.9 copy-done.7
  112.4 30.2 %share_rows.1 = (bf16[16,128,256]{2,1,0:T(8,128)(2,1)S(1)}, f32[2,128,256]{2,1,0:T(8,128)S(1)}) custom-call(bf16[16,2,128,256]{3,2,1,0:T(8,128)(2,1)S(1)} %bitcast.16, f32[128,256]{1,0:T(8,128)S(1)} %copy-done.7), custom_call_target="tpu_custom_call" | custom-call | tf_op jit(solution)/shard_map/share_rows/pallas_call | solution.py:501
  142.7 0.0 copy-start.4
  142.7 1.0 copy-done.4
  143.6 0.7 copy-done.6
  144.4 42.4 %solve.1 = (bf16[32,128,256]{2,1,0:T(8,128)(2,1)}, bf16[16,128,256]{2,1,0:T(8,128)(2,1)}, f32[32,128,256]{2,1,0:T(8,128)}, f32[8,128]{1,0:T(8,128)}) custom-call(f32[2,128,256]{2,1,0:T(8,128)} %copy-done.6, bf16[32,128,256]{2,1,0:T(8,128)(2,1)} %get-tuple-element.18.dense, bf16[16,128,256]{2,1,0:T(8,128)(2,1)} %copy-done.4), custom_call_target="tpu_custom_call" | custom-call | tf_op jit(solution)/shard_map/solve/pallas_call | solution.py:516
  186.8 1.2 slice.3
  188.0 0.0 copy-done.9
  188.0 0.6 dynamic-slice
  189.2 0.0 collective-permute-done
  189.2 3.2 %collective-permute-start.3 = (bf16[1,2,512,128]{3,2,1,0:T(8,128)(2,1)S(1)}, bf16[1,2,512,128]{3,2,1,0:T(8,128)(2,1)S(1)}, u32[]{:S(2)}, u32[]{:S(2)}) collective-permute-start(bf16[1,2,512,128]{3,2,1,0:T(8,128)(2,1)S(1)} %get-tuple-element.45), channel_id=1, source_target_pairs={{0,4},{1,5},{2,6},{3,7},{4,0},{5,1},{6,2},{7,3},{8,12},{9,13},{10,... | collective-permute-start | bytes 786440 | tf_op jit(solution)/shard_map/ppermute | solution.py:484
  192.5 1.0 constant_dynamic-update-slice_fusion.6
  193.5 0.0 collective-permute-done.1
  193.5 0.6 collective-permute-start.4
  194.0 1.0 constant_dynamic-update-slice_fusion.5
  195.0 0.0 collective-permute-done.2
  195.0 1.0 constant_dynamic-update-slice_fusion.4
  196.0 9.0 %collective-permute-done.3 = bf16[1,2,512,128]{3,2,1,0:T(8,128)(2,1)S(1)} collective-permute-done((bf16[1,2,512,128]{3,2,1,0:T(8,128)(2,1)S(1)}, bf16[1,2,512,128]{3,2,1,0:T(8,128)(2,1)S(1)}, u32[]{:S(2)}, u32[]{:S(2)}) %collective-permute-start.3) | collective-permute-done | bytes 262176 | tf_op jit(solution)/shard_map/ppermute | solution.py:484
  205.1 0.0 collective-permute-done.4
  205.1 0.0 collective-permute-done.5
  205.1 1.0 constant_dynamic-update-slice_fusion.1
  206.1 0.0 collective-permute-done.6
  206.1 1.0 constant_dynamic-update-slice_fusion.tiles
  207.1 0.0 copy-start.8
  207.1 1.3 copy-done.8
  208.5 37.0 %final.1 = (f32[32,2048,128]{2,1,0:T(8,128)}, bf16[32,2048,128]{2,1,0:T(8,128)(2,1)}, f32[16,128]{1,0:T(8,128)}) custom-call(s32[2]{0:T(128)} %pad_add_fusion.ids, s32[8,16]{1,0:T(8,128)} %blocks.7, bf16[32,128,256]{2,1,0:T(8,128)(2,1)} %get-tuple-element.22.rows_ref, bf16[16,128,256]{2,1,0:T(8,128)(2,1)} %get-tuple-element.23.cols_ref, ...), custom_call_target="tpu_custom_call" | custom-call | tf_op jit(solution)/shard_map/final/pallas_call | solution.py:533
  245.4 10.3 %all-reduce = f32[2048]{0:T(1024)S(1)} all-reduce(f32[2048]{0:T(1024)} %bitcast.19), channel_id=2, replica_groups=mesh['row'=4,'col'=8] {'row'}, use_global_device_ids=true, to_apply=%region_0.0.clone | all-reduce | flops 2048 | bytes 16384
  255.8 0.7 dynamic-slice.1
  (8 shorter events, 0.1 us)
Async XLA Ops:
  5.8 1.2 copy-start.3
  39.4 1.8 copy-start
  53.2 9.0 %copy-start.5 = (bf16[512,256]{1,0:T(8,128)(2,1)S(1)}, bf16[512,256]{1,0:T(8,128)(2,1)}, u32[]{:S(2)}) copy-start(bf16[512,256]{1,0:T(8,128)(2,1)} %get-tuple-element.17.mine) | copy-start | bytes 786436
  55.8 133.4 %collective-permute-start = (bf16[1,2,512,128]{3,2,1,0:T(8,128)(2,1)}, bf16[1,2,512,128]{3,2,1,0:T(8,128)(2,1)}, u32[]{:S(2)}, u32[]{:S(2)}) collective-permute-start(bf16[1,2,512,128]{3,2,1,0:T(8,128)(2,1)} %get-tuple-element.48), channel_id=1, source_target_pairs={{0,1},{1,2},{2,3},{3,4},{4,5},{5,6},{6,7},{7,0},{8,9},{9,10},{10,1... | collective-permute-start | bytes 786440 | tf_op jit(solution)/shard_map/ppermute | solution.py:484
  55.8 137.7 %collective-permute-start.1 = (bf16[1,2,512,128]{3,2,1,0:T(8,128)(2,1)}, bf16[1,2,512,128]{3,2,1,0:T(8,128)(2,1)}, u32[]{:S(2)}, u32[]{:S(2)}) collective-permute-start(bf16[1,2,512,128]{3,2,1,0:T(8,128)(2,1)} %get-tuple-element.47), channel_id=1, source_target_pairs={{0,2},{1,3},{2,4},{3,5},{4,6},{5,7},{6,0},{7,1},{8,10},{9,11},{10,... | collective-permute-start | bytes 786440 | tf_op jit(solution)/shard_map/ppermute | solution.py:484
  57.4 137.6 %collective-permute-start.2 = (bf16[1,2,512,128]{3,2,1,0:T(8,128)(2,1)S(1)}, bf16[1,2,512,128]{3,2,1,0:T(8,128)(2,1)}, u32[]{:S(2)}, u32[]{:S(2)}) collective-permute-start(bf16[1,2,512,128]{3,2,1,0:T(8,128)(2,1)S(1)} %get-tuple-element.46), channel_id=1, source_target_pairs={{0,3},{1,4},{2,5},{3,6},{4,7},{5,0},{6,1},{7,2},{8,11},{9,12},{10,... | collective-permute-start | bytes 786440 | tf_op jit(solution)/shard_map/ppermute | solution.py:484
  59.9 146.2 %collective-permute-start.6 = (bf16[1,2,512,128]{3,2,1,0:T(8,128)(2,1)S(1)}, bf16[1,2,512,128]{3,2,1,0:T(8,128)(2,1)}, u32[]{:S(2)}, u32[]{:S(2)}) collective-permute-start(bf16[1,2,512,128]{3,2,1,0:T(8,128)(2,1)S(1)} %get-tuple-element.42), channel_id=1, source_target_pairs={{0,7},{1,0},{2,1},{3,2},{4,3},{5,4},{6,5},{7,6},{8,15},{9,8},{10,9... | collective-permute-start | bytes 786440 | tf_op jit(solution)/shard_map/ppermute | solution.py:484
  61.0 144.1 %collective-permute-start.5 = (bf16[1,2,512,128]{3,2,1,0:T(8,128)(2,1)S(1)}, bf16[1,2,512,128]{3,2,1,0:T(8,128)(2,1)}, u32[]{:S(2)}, u32[]{:S(2)}) collective-permute-start(bf16[1,2,512,128]{3,2,1,0:T(8,128)(2,1)S(1)} %get-tuple-element.43), channel_id=1, source_target_pairs={{0,6},{1,7},{2,0},{3,1},{4,2},{5,3},{6,4},{7,5},{8,14},{9,15},{10,... | collective-permute-start | bytes 786440 | tf_op jit(solution)/shard_map/ppermute | solution.py:484
  104.7 1.3 copy-start.1
  110.0 1.6 copy-start.2
  111.5 0.9 copy-start.7
  142.7 1.0 copy-start.4
  143.6 0.7 copy-start.6
  144.4 43.6 %copy-start.9 = (u32[32]{0:T(128)S(1)}, u32[32]{0:T(128)}, u32[]{:S(2)}) copy-start(u32[32]{0:T(128)} %constant.44) | copy-start | bytes 388
  189.2 15.8 %collective-permute-start.3 = (bf16[1,2,512,128]{3,2,1,0:T(8,128)(2,1)S(1)}, bf16[1,2,512,128]{3,2,1,0:T(8,128)(2,1)S(1)}, u32[]{:S(2)}, u32[]{:S(2)}) collective-permute-start(bf16[1,2,512,128]{3,2,1,0:T(8,128)(2,1)S(1)} %get-tuple-element.45), channel_id=1, source_target_pairs={{0,4},{1,5},{2,6},{3,7},{4,0},{5,1},{6,2},{7,3},{8,12},{9,13},{10,... | collective-permute-start | bytes 786440 | tf_op jit(solution)/shard_map/ppermute | solution.py:484
  193.5 11.6 %collective-permute-start.4 = (bf16[1,2,512,128]{3,2,1,0:T(8,128)(2,1)S(1)}, bf16[1,2,512,128]{3,2,1,0:T(8,128)(2,1)S(1)}, u32[]{:S(2)}, u32[]{:S(2)}) collective-permute-start(bf16[1,2,512,128]{3,2,1,0:T(8,128)(2,1)S(1)} %get-tuple-element.44), channel_id=1, source_target_pairs={{0,5},{1,6},{2,7},{3,0},{4,1},{5,2},{6,3},{7,4},{8,13},{9,14},{10,... | collective-permute-start | bytes 786440 | tf_op jit(solution)/shard_map/ppermute | solution.py:484
  207.1 1.4 copy-start.8

commit v2 on v1

--- a/solution.py
+++ b/solution.py
@@ -214,13 +214,24 @@
     dense[...] = work[...].astype(jnp.bfloat16)
 
 
-def share_rows_kernel(rows_n, dense, corner, cols, corners, sends, recvs, csends, crecvs, local):
+def share_rows_kernel(
+    rows_n, cols_n, near_n, dense, corner, strips, cols, corners, near,
+    sends, recvs, csends, crecvs, local, nsends, nrecvs
+):
     row = lax.axis_index("row")
     col = lax.axis_index("col")
     ratio_part = col // rows_n
     owner = lax.rem(col, rows_n)
     peers = [(lax.rem(row + k, rows_n), col) for k in range(1, rows_n)]
-    greet(peers)
+    greet(peers + [(row, lax.rem(col - k + cols_n, cols_n)) for k in range(1, near_n + 1)])
+    tiles = []
+    for k in range(1, near_n + 1):
+        target = lax.rem(col + k, cols_n)
+        tiles.append(
+            remote(
+                strips.at[target], near.at[k - 1], nsends.at[k - 1], nrecvs.at[k - 1], (row, target)
+            )
+        )
     for b in range(PANEL_BLOCKS):
 
         @pl.when(row == b)
@@ -235,6 +246,8 @@
             remote(dense.at[:, ratio_part], cols, sends.at[k], recvs.at[0], peer).start()
         pltpu.make_async_copy(dense.at[:, ratio_part], cols, local.at[1]).start()
 
+    for job in tiles:
+        job.start()
     for b in range(PANEL_BLOCKS):
 
         @pl.when(row == b)
@@ -257,6 +270,9 @@
     def _():
         remote(dense.at[:, ratio_part], cols, sends.at[0], recvs.at[0], peers[0]).wait_recv()
 
+    for job in tiles:
+        job.wait()
+
 
 def eliminate(work, tile):
     first = lax.broadcasted_iota(jnp.int32, (tile, tile), 0)
@@ -264,15 +280,42 @@
     lane = lax.broadcasted_iota(jnp.int32, (1, tile), 1)
     sub = lax.broadcasted_iota(jnp.int32, (tile, 1), 0)
 
-    @pl.loop(0, tile)
-    def _(j):
+    many = 4
+
+    @pl.loop(0, tile // many)
+    def _(step):
+        start = step * many
         now = work[...]
-        line = work[pl.ds(j, 1), :]
-        pivot = jnp.sum(jnp.where(lane == j, line, 0.0), axis=1, keepdims=True)
-        column = jnp.sum(jnp.where(second == j, now, 0.0), axis=1, keepdims=True)
-        factor = jnp.where(sub > j, column / pivot, 0.0)
-        base = jnp.where((second == j) & (first > j), 0.0, now)
-        work[...] = base - factor * jnp.where(lane == j, 1.0, line)
+        rows = [work[pl.ds(start + a, 1), :] for a in range(many)]
+        cols = [
+            jnp.sum(jnp.where(second == start + a, now, 0.0), axis=1, keepdims=True)
+            for a in range(many)
+        ]
+        small = [
+            [
+                jnp.sum(jnp.where(lane == start + b, rows[a], 0.0), axis=1, keepdims=True)
+                for b in range(many)
+            ]
+            for a in range(many)
+        ]
+        after = sub >= start + many
+        inside = (second >= start) & (second < start + many) & (first >= start + many)
+        base = jnp.where(inside, 0.0, now)
+        for a in range(many):
+            inv = 1.0 / small[a][a]
+            fixed = jnp.where(lane == start + a, 1.0, rows[a])
+            scale = jnp.where(after, cols[a] * inv, 0.0)
+            below = (lane > start + a) & (lane < start + many)
+            base = base - scale * jnp.where(below, 0.0, fixed)
+            for b in range(a + 1, many):
+                ratio = small[b][a] * inv
+                rows[b] = jnp.where(lane == start + a, 0.0, rows[b]) - ratio * fixed
+                cols[b] = cols[b] - scale * small[a][b]
+                for c in range(a + 1, many):
+                    small[b][c] = small[b][c] - ratio * small[a][c]
+        work[...] = base
+        for a in range(1, many):
+            work[pl.ds(start + a, 1), :] = rows[a]
 
     done = work[...]
     eye = first == second
@@ -310,24 +353,24 @@
         rows_out[i] = got.astype(jnp.bfloat16)
         exact[i] = got
 
-    @pl.loop(0, cols.shape[0])
-    def _(i):
-        cols_out[i] = apply(cols[i]).astype(jnp.bfloat16)
+    for i in range(cols.shape[0]):
+        got = dot_nt(high, cols[i], None) + dot_nt(low, cols[i], None)
+        cols_out[:, pl.ds(i * tile, tile)] = got.astype(jnp.bfloat16)
 
 
 def final_kernel(
-    per_row, slots, rows_n, cols_n, ids, blocks, rows_ref, cols_ref, own_ref, tiles,
+    per_row, slots, rows_n, cols_n, batch, ids, blocks, rows_ref, cols_ref, own_ref, tiles,
     full, corr, diag, upd, col_tab, row_cnt, row_tab
 ):
-    i = pl.program_id(0)
-    nb_r = pl.num_programs(0)
+    first = pl.program_id(0) * batch
+    nb_r = pl.num_programs(0) * batch
     tile = rows_ref.shape[1]
-    nb_c = cols_ref.shape[0]
+    nb_c = cols_ref.shape[1] // tile
     kcount = blocks.shape[1]
     row = ids[0]
     col = ids[1]
 
-    @pl.when(i == 0)
+    @pl.when(first == 0)
     def _():
         diag[...] = jnp.zeros_like(diag)
 
@@ -358,57 +401,67 @@
                 row_cnt[place] = n + 1
                 row_tab[place * cols_n + n] = c * (cols_n * per_row) + shift * per_row + j
 
-    above = i * rows_n + row < PANEL_BLOCKS
-    left = rows_ref[0]
-    for jj in range(nb_c):
-        upd[pl.ds(jj, tile, stride=nb_c), :] = dot_nt(left, cols_ref[jj], None)
-    in_panel = col < PANEL_BLOCKS
-    place = lax.rem(lax.broadcasted_iota(jnp.int32, (tile * nb_c, upd.shape[1]), 0), nb_c)
-
-    @pl.when(above)
-    def _():
-        corr[0] = jnp.zeros(corr.shape[1:], corr.dtype)
-        full[0] = jnp.zeros(full.shape[1:], full.dtype)
-
-    @pl.when(jnp.logical_not(above))
-    def _():
-        value = upd[...]
-        full[0] = -value
-        corr[0] = jnp.where((place == 0) & in_panel, 0.0, value).astype(corr.dtype)
-
-        @pl.loop(0, row_cnt[i])
-        def _(n):
-            code = row_tab[i * cols_n + n]
-            c = code // (cols_n * per_row)
-            rest = lax.rem(code, cols_n * per_row)
-            shift = rest // per_row
-            j = lax.rem(rest, per_row)
-            for s in range(slots):
-                jj = col_tab[c * slots + s]
-
-                @pl.when(jj >= 0)
-                def _():
-                    part = tiles[shift, s, pl.ds(pl.multiple_of(j * tile, tile), tile), :]
-                    where = pl.ds(jj, tile, stride=nb_c)
-                    full[0, where, :] = full[0, where, :] + part.astype(jnp.float32)
-
-    @pl.when(in_panel)
-    def _():
-        full[0, pl.ds(0, tile, stride=nb_c), :] = own_ref[0]
-
-    far = i * rows_n + row - col
-
-    @pl.when((far >= 0) & (lax.rem(far + cols_n * nb_c, cols_n) == 0))
-    def _():
-        jj = far // cols_n
-        where = pl.ds(jj, tile, stride=nb_c)
-        block = full[0, where, :]
-        eye = lax.broadcasted_iota(jnp.int32, block.shape, 0) == lax.broadcasted_iota(
-            jnp.int32, block.shape, 1
+    left = rows_ref[...].reshape(batch * tile, rows_ref.shape[2])
+    pair = 2
+    for jj in range(0, nb_c, pair):
+        got = jnp.dot(
+            left, cols_ref[:, pl.ds(jj * tile, pair * tile)], preferred_element_type=jnp.float32
         )
-        full[0, where, :] = jnp.where(eye, 0.0, block)
-        prior = jnp.where(jnp.logical_or(above, in_panel & (jj == 0)), 0.0, item_prior)
-        diag[pl.ds(jj, 1), :] = jnp.sum(jnp.where(eye, block, 0.0), axis=0, keepdims=True) + prior
+        for u in range(batch):
+            for v in range(pair):
+                part = got[u * tile : (u + 1) * tile, v * tile : (v + 1) * tile]
+                upd[u, pl.ds(jj + v, tile, stride=nb_c), :] = part
+
+    for u in range(batch):
+        i = first + u
+        above = i * rows_n + row < PANEL_BLOCKS
+        in_panel = col < PANEL_BLOCKS
+        place = lax.rem(lax.broadcasted_iota(jnp.int32, (tile * nb_c, upd.shape[2]), 0), nb_c)
+
+        @pl.when(above)
+        def _():
+            corr[u] = jnp.zeros(corr.shape[1:], corr.dtype)
+            full[u] = jnp.zeros(full.shape[1:], full.dtype)
+
+        @pl.when(jnp.logical_not(above))
+        def _():
+            value = upd[u]
+            full[u] = -value
+            corr[u] = jnp.where((place == 0) & in_panel, 0.0, value).astype(corr.dtype)
+
+            @pl.loop(0, row_cnt[i])
+            def _(n):
+                code = row_tab[i * cols_n + n]
+                c = code // (cols_n * per_row)
+                rest = lax.rem(code, cols_n * per_row)
+                shift = rest // per_row
+                j = lax.rem(rest, per_row)
+                for s in range(slots):
+                    jj = col_tab[c * slots + s]
+
+                    @pl.when(jj >= 0)
+                    def _():
+                        part = tiles[shift, s, pl.ds(pl.multiple_of(j * tile, tile), tile), :]
+                        where = pl.ds(jj, tile, stride=nb_c)
+                        full[u, where, :] = full[u, where, :] + part.astype(jnp.float32)
+
+        @pl.when(in_panel)
+        def _():
+            full[u, pl.ds(0, tile, stride=nb_c), :] = own_ref[u]
+
+        far = i * rows_n + row - col
+
+        @pl.when((far >= 0) & (lax.rem(far + cols_n * nb_c, cols_n) == 0))
+        def _():
+            jj = far // cols_n
+            where = pl.ds(jj, tile, stride=nb_c)
+            block = full[u, where, :]
+            eye = lax.broadcasted_iota(jnp.int32, block.shape, 0) == lax.broadcasted_iota(
+                jnp.int32, block.shape, 1
+            )
+            full[u, where, :] = jnp.where(eye, 0.0, block)
+            prior = jnp.where(jnp.logical_or(above, in_panel & (jj == 0)), 0.0, item_prior)
+            diag[pl.ds(jj, 1), :] = jnp.sum(jnp.where(eye, block, 0.0), axis=0, keepdims=True) + prior
 
 
 def params(limit=BIG, **kw):
@@ -477,12 +530,13 @@
         name="gather_cols",
     )(panel)
 
+    strips, gathered = lax.optimization_barrier((strips, gathered))
     strips = strips.reshape(cols_n, slots, group, tile)
+    near_n = min(3, cols_n - 1)
     parts = [lax.dynamic_slice_in_dim(strips, col_idx, 1, 0)]
-    for k in range(1, cols_n):
+    for k in range(near_n + 1, cols_n):
         part = lax.dynamic_slice_in_dim(strips, lax.rem(col_idx + k, cols_n), 1, 0)
         parts.append(lax.ppermute(part, "col", [(c, (c + k) % cols_n) for c in range(cols_n)]))
-    tiles = jnp.concatenate(parts, axis=0)
 
     dense, corner = pl.pallas_call(
         functools.partial(dense_kernel, per_row, tile, rows_n),
@@ -498,26 +552,29 @@
     )(ids, block_list, gathered)
 
     ratio = cols_n // rows_n
-    panel_cols, corners = pl.pallas_call(
-        functools.partial(share_rows_kernel, rows_n),
+    panel_cols, corners, near = pl.pallas_call(
+        functools.partial(share_rows_kernel, rows_n, cols_n, near_n),
         out_shape=(
             jax.ShapeDtypeStruct((nb_c, tile, width_p), bf16),
             jax.ShapeDtypeStruct((PANEL_BLOCKS, tile, width_p), f32),
+            jax.ShapeDtypeStruct((near_n, slots, group, tile), bf16),
         ),
-        in_specs=[HBM, HBM],
-        out_specs=(HBM, HBM),
+        in_specs=[HBM, HBM, HBM],
+        out_specs=(HBM, HBM, HBM),
         scratch_shapes=[
             dma((rows_n,)), dma((1,)), dma((rows_n,)), dma((PANEL_BLOCKS,)), dma((2,)),
+            dma((near_n,)), dma((near_n,)),
         ],
         compiler_params=params(2**20, collective_id=2, has_side_effects=True),
         name="share_rows",
-    )(dense.reshape(nb_c, ratio, tile, width_p), corner)
+    )(dense.reshape(nb_c, ratio, tile, width_p), corner, strips)
+    tiles = jnp.concatenate([parts[0], near] + parts[1:], axis=0)
 
     rows_f, cols_f, exact, logs = pl.pallas_call(
         functools.partial(solve_kernel, tile),
         out_shape=(
             jax.ShapeDtypeStruct((nb_r, tile, width_p), bf16),
-            jax.ShapeDtypeStruct((nb_c, tile, width_p), bf16),
+            jax.ShapeDtypeStruct((width_p, nb_c * tile), bf16),
             jax.ShapeDtypeStruct((nb_r, tile, width_p), f32),
             jax.ShapeDtypeStruct((8, tile), f32),
         ),
@@ -530,26 +587,27 @@
     logdet = logs[0, 0]
 
     rows_all = tile * nb_c
+    batch = 2
     full, corr, diag = pl.pallas_call(
-        functools.partial(final_kernel, per_row, slots, rows_n, cols_n),
+        functools.partial(final_kernel, per_row, slots, rows_n, cols_n, batch),
         grid_spec=pltpu.PrefetchScalarGridSpec(
             num_scalar_prefetch=2,
-            grid=(nb_r,),
+            grid=(nb_r // batch,),
             in_specs=[
-                pl.BlockSpec((1, tile, width_p), lambda i, ids, bl: (i, 0, 0)),
-                pl.BlockSpec((nb_c, tile, width_p), lambda i, ids, bl: (0, 0, 0)),
+                pl.BlockSpec((batch, tile, width_p), lambda i, ids, bl: (i, 0, 0)),
+                pl.BlockSpec((width_p, nb_c * tile), lambda i, ids, bl: (0, 0)),
                 pl.BlockSpec(
-                    (1, tile, tile), lambda i, ids, bl: (i, 0, jnp.minimum(ids[1], PANEL_BLOCKS - 1))
+                    (batch, tile, tile), lambda i, ids, bl: (i, 0, jnp.minimum(ids[1], PANEL_BLOCKS - 1))
                 ),
                 pl.BlockSpec((cols_n, slots, group, tile), lambda i, ids, bl: (0, 0, 0, 0)),
             ],
             out_specs=[
-                pl.BlockSpec((1, rows_all, tile), lambda i, ids, bl: (i, 0, 0)),
-                pl.BlockSpec((1, rows_all, tile), lambda i, ids, bl: (i, 0, 0)),
+                pl.BlockSpec((batch, rows_all, tile), lambda i, ids, bl: (i, 0, 0)),
+                pl.BlockSpec((batch, rows_all, tile), lambda i, ids, bl: (i, 0, 0)),
                 pl.BlockSpec((nb_c, tile), lambda i, ids, bl: (0, 0)),
             ],
             scratch_shapes=[
-                pltpu.VMEM((rows_all, tile), f32),
+                pltpu.VMEM((batch, rows_all, tile), f32),
                 pltpu.SMEM((cols_n * slots,), jnp.int32),
                 pltpu.SMEM((nb_r,), jnp.int32),
                 pltpu.SMEM((nb_r * cols_n,), jnp.int32),

time: 259 us -> 204 us (0.79)
  Pallas kernels: 204 us -> 162 us
  waiting for transfers between devices: 9.04 us -> 0.01 us
    pallas_call x1, Pallas kernels: 42.5 us -> 23.7 us  [body(): pl.pallas_call(functools.partial(gather_cols_kernel, cols_n), out_shape=j...]
    pallas_call x1, Pallas kernels: 42.4 us -> 25.3 us  [body(): pl.pallas_call(functools.partial(solve_kernel, tile), out_shape=(jax.Shap...]
    ppermute x7 -> x4, waiting for transfers between devices: 9.04 us -> 0.01 us  [body(): lax.ppermute(part, 'col', [(c, (c + k) % cols_n) for c in range(cols_n)])]
    pallas_call x1, Pallas kernels: 37 us -> 29.6 us  [body(): pl.pallas_call(functools.partial(final_kernel, per_row, slots, rows_n, co...]
    ppermute x7 -> x4, starting transfers between devices: 10.2 us -> 9.86 us  [body(): lax.ppermute(part, 'col', [(c, (c + k) % cols_n) for c in range(cols_n)])]
  transfers between devices with their start and end apart: 7 -> 4, of which waited for: 1 -> 0; matrix products, arithmetic and copies ran while one was open for 2% -> 3% of each run, Pallas kernels for 46% -> 30%
where the time goes in v2:
time: 204 us; the launch traced here: 203 us
  Pallas kernels  162 us (79%)
  local copies, waits for them, and re-layouts  20.7 us (10%)
  starting transfers between devices  9.86 us (5%)
  blocking collectives  8.42 us (4%)
    pallas_call x1, Pallas kernels, body(): pl.pallas_call(functools.partial(gather_rows_kernel, rows_n), out_shape=j...  32.4 us
    pallas_call x1, Pallas kernels, body(): pl.pallas_call(functools.partial(share_rows_kernel, rows_n, cols_n, near_...  32.2 us
    pallas_call x1, Pallas kernels, body(): pl.pallas_call(functools.partial(final_kernel, per_row, slots, rows_n, co...  29.6 us
    pallas_call x1, Pallas kernels, body(): pl.pallas_call(functools.partial(solve_kernel, tile), out_shape=(jax.Shap...  25.3 us
    pallas_call x1, Pallas kernels, body(): pl.pallas_call(functools.partial(gather_cols_kernel, cols_n), out_shape=j...  23.7 us
    unnamed x28, local copies, waits for them, and re-layouts  17.2 us
    pallas_call x1, Pallas kernels, body(): pl.pallas_call(functools.partial(product_kernel, per_row, tile, rows_n, c...  12.1 us
    ppermute x4, starting transfers between devices, body(): lax.ppermute(part, 'col', [(c, (c + k) % cols_n) for c in range(cols_n)])  9.86 us
  transfers between devices with their start and end apart: 4, of which 0 were waited for; matrix products, arithmetic and copies ran while one was open for 3% of the time, Pallas kernels for 30%

profile of v2, /device:TPU:0, one launch (start us, length us, event | category | flops | bytes accessed | tf_op | source)
XLA Modules:
  0.0 203.2 jit_solution(15194812563634335792)
XLA Ops:
  0.7 1.4 copy.13.effect
  2.1 0.6 pad_add_fusion.ids
  2.7 3.1 %weights.1.mine = bf16[208,2048]{1,0:T(8,128)(2,1)} custom-call(s32[2]{0:T(128)} %pad_add_fusion.ids, s32[8,16]{1,0:T(8,128)} %blocks.7, s32[192,2048]{1,0:T(8,128)} %bitcast.19, f32[192,1]{1,0:T(8,128)} %copy.13.effect, f32[128,128]{1,0:T(8,128)} %items.1), custom_call_target="tpu_custom_call" | custom-call | tf_op jit(solution)/shard_map/weights/pallas_call | solution.py:490
  5.8 0.0 copy-start.4
  5.8 1.2 copy-done.4
  6.9 32.4 %gather_rows.1.stacked = bf16[4,208,2048]{2,1,0:T(8,128)(2,1)S(1)} custom-call(bf16[208,2048]{1,0:T(8,128)(2,1)S(1)} %copy-done.4), custom_call_target="tpu_custom_call" | custom-call | tf_op jit(solution)/shard_map/gather_rows/pallas_call | solution.py:500
  39.3 0.0 copy-start
  39.3 1.7 copy-done
  41.1 12.1 %products.1 = (bf16[16,512,128]{2,1,0:T(8,128)(2,1)}, bf16[512,256]{1,0:T(8,128)(2,1)}) custom-call(s32[2]{0:T(128)} %pad_add_fusion.ids, s32[8,16]{1,0:T(8,128)} %blocks.7, bf16[4,208,2048]{2,1,0:T(8,128)(2,1)} %copy-done), custom_call_target="tpu_custom_call" | custom-call | tf_op jit(solution)/shard_map/products/pallas_call | solution.py:510
  53.2 0.0 copy-start.3
  53.2 1.1 copy-done.6
  54.3 23.7 %gather_cols.1.gathered = bf16[8,512,256]{2,1,0:T(8,128)(2,1)S(1)} custom-call(bf16[512,256]{1,0:T(8,128)(2,1)S(1)} %copy-done.6), custom_call_target="tpu_custom_call" | custom-call | tf_op jit(solution)/shard_map/gather_cols/pallas_call | solution.py:523
  78.0 0.0 copy-start.1
  78.0 1.3 copy-done.1
  79.3 0.0 copy-done.3
  79.3 0.1 constant_dynamic-slice_fusion
  79.4 2.6 %collective-permute-start = (bf16[1,2,512,128]{3,2,1,0:T(8,128)(2,1)S(1)}, bf16[1,2,512,128]{3,2,1,0:T(8,128)(2,1)}, u32[]{:S(2)}, u32[]{:S(2)}) collective-permute-start(bf16[1,2,512,128]{3,2,1,0:T(8,128)(2,1)S(1)} %get-tuple-element.51), channel_id=1, source_target_pairs={{0,4},{1,5},{2,6},{3,7},{4,0},{5,1},{6,2},{7,3},{8,12},{9,13},{10,... | collective-permute-start | bytes 786440 | tf_op jit(solution)/shard_map/ppermute | solution.py:539
  82.0 0.1 collective-permute-start.1
  82.1 4.1 %collective-permute-start.3 = (bf16[1,2,512,128]{3,2,1,0:T(8,128)(2,1)S(1)}, bf16[1,2,512,128]{3,2,1,0:T(8,128)(2,1)S(1)}, u32[]{:S(2)}, u32[]{:S(2)}) collective-permute-start(bf16[1,2,512,128]{3,2,1,0:T(8,128)(2,1)S(1)} %get-tuple-element.48), channel_id=1, source_target_pairs={{0,7},{1,0},{2,1},{3,2},{4,3},{5,4},{6,5},{7,6},{8,15},{9,8},{10,9... | collective-permute-start | bytes 786440 | tf_op jit(solution)/shard_map/ppermute | solution.py:539
  86.2 3.0 %collective-permute-start.2 = (bf16[1,2,512,128]{3,2,1,0:T(8,128)(2,1)S(1)}, bf16[1,2,512,128]{3,2,1,0:T(8,128)(2,1)}, u32[]{:S(2)}, u32[]{:S(2)}) collective-permute-start(bf16[1,2,512,128]{3,2,1,0:T(8,128)(2,1)S(1)} %get-tuple-element.49), channel_id=1, source_target_pairs={{0,6},{1,7},{2,0},{3,1},{4,2},{5,3},{6,4},{7,5},{8,14},{9,15},{10,... | collective-permute-start | bytes 786440 | tf_op jit(solution)/shard_map/ppermute | solution.py:539
  89.2 3.9 %dense.1 = (bf16[32,128,256]{2,1,0:T(8,128)(2,1)}, f32[128,256]{1,0:T(8,128)}) custom-call(s32[2]{0:T(128)} %pad_add_fusion.ids, s32[8,16]{1,0:T(8,128)} %blocks.7, bf16[8,512,256]{2,1,0:T(8,128)(2,1)} %copy-done.1), custom_call_target="tpu_custom_call" | custom-call | tf_op jit(solution)/shard_map/dense/pallas_call | solution.py:541
  93.1 0.0 copy-start.2
  93.1 1.6 copy-done.2
  94.7 0.0 copy-start.8
  94.7 0.9 copy-done.8
  95.6 32.2 %share_rows.1 = (bf16[16,128,256]{2,1,0:T(8,128)(2,1)S(1)}, f32[2,128,256]{2,1,0:T(8,128)S(1)}, bf16[3,2,512,128]{3,2,1,0:T(8,128)(2,1)S(1)}) custom-call(bf16[16,2,128,256]{3,2,1,0:T(8,128)(2,1)S(1)} %bitcast.16, f32[128,256]{1,0:T(8,128)S(1)} %copy-done.8, bf16[8,2,512,128]{3,2,1,0:T(8,128)(2,1)S(1)} %bitcast.18), custom_call_target="tpu_custom_call" | custom-call | tf_op jit(solution)/shard_map/share_rows/pallas_call | solution.py:555
  127.9 0.0 copy-start.5
  127.9 1.0 copy-done.5
  128.9 0.0 copy-start.7
  128.9 0.7 copy-done.7
  129.6 0.1 constant_dynamic-update-slice_fusion.4
  129.7 0.0 copy-start.9
  129.7 1.4 copy-done.9
  131.0 25.3 %solve.1 = (bf16[32,128,256]{2,1,0:T(8,128)(2,1)}, bf16[256,2048]{1,0:T(8,128)(2,1)}, f32[32,128,256]{2,1,0:T(8,128)}, f32[8,128]{1,0:T(8,128)}) custom-call(f32[2,128,256]{2,1,0:T(8,128)} %copy-done.7, bf16[32,128,256]{2,1,0:T(8,128)(2,1)} %get-tuple-element.23.dense, bf16[16,128,256]{2,1,0:T(8,128)(2,1)} %copy-done.5), custom_call_target="tpu_custom_call" | custom-call | tf_op jit(solution)/shard_map/solve/pallas_call | solution.py:573
  156.3 1.2 slice.3
  157.5 0.0 copy-done.10
  157.5 0.6 dynamic-slice
  158.8 0.0 collective-permute-done
  158.8 1.7 constant_dynamic-update-slice_fusion.3
  160.4 0.0 collective-permute-done.1
  160.4 1.7 constant_dynamic-update-slice_fusion.2
  162.1 0.0 collective-permute-done.2
  162.1 1.7 constant_dynamic-update-slice_fusion.1
  163.8 0.0 collective-permute-done.3
  163.8 0.7 constant_dynamic-update-slice_fusion.tiles
  164.6 29.6 %final.1 = (f32[32,2048,128]{2,1,0:T(8,128)}, bf16[32,2048,128]{2,1,0:T(8,128)(2,1)}, f32[16,128]{1,0:T(8,128)}) custom-call(s32[2]{0:T(128)} %pad_add_fusion.ids, s32[8,16]{1,0:T(8,128)} %blocks.7, bf16[32,128,256]{2,1,0:T(8,128)(2,1)} %get-tuple-element.28.rows_ref, bf16[256,2048]{1,0:T(8,128)(2,1)} %get-tuple-element.29.cols_ref, ...), custom_call_target="tpu_custom_call" | custom-call | tf_op jit(solution)/shard_map/final/pallas_call | solution.py:591
  194.1 8.4 %all-reduce = f32[2048]{0:T(1024)S(1)} all-reduce(f32[2048]{0:T(1024)} %bitcast.20), channel_id=2, replica_groups=mesh['row'=4,'col'=8] {'row'}, use_global_device_ids=true, to_apply=%region_0.0.clone | all-reduce | flops 2048 | bytes 16384
  202.5 0.7 dynamic-slice.1
  (2 shorter events, 0.0 us)
Async XLA Ops:
  5.8 1.2 copy-start.4
  39.3 1.8 copy-start
  53.2 26.1 %copy-start.3 = (bf16[16,512,128]{2,1,0:T(8,128)(2,1)S(1)}, bf16[16,512,128]{2,1,0:T(8,128)(2,1)}, u32[]{:S(2)}) copy-start(bf16[16,512,128]{2,1,0:T(8,128)(2,1)} %get-tuple-element.25) | copy-start | bytes 6291460
  53.2 1.1 copy-start.6
  78.0 1.3 copy-start.1
  79.4 79.4 %collective-permute-start = (bf16[1,2,512,128]{3,2,1,0:T(8,128)(2,1)S(1)}, bf16[1,2,512,128]{3,2,1,0:T(8,128)(2,1)}, u32[]{:S(2)}, u32[]{:S(2)}) collective-permute-start(bf16[1,2,512,128]{3,2,1,0:T(8,128)(2,1)S(1)} %get-tuple-element.51), channel_id=1, source_target_pairs={{0,4},{1,5},{2,6},{3,7},{4,0},{5,1},{6,2},{7,3},{8,12},{9,13},{10,... | collective-permute-start | bytes 786440 | tf_op jit(solution)/shard_map/ppermute | solution.py:539
  82.0 78.5 %collective-permute-start.1 = (bf16[1,2,512,128]{3,2,1,0:T(8,128)(2,1)S(1)}, bf16[1,2,512,128]{3,2,1,0:T(8,128)(2,1)}, u32[]{:S(2)}, u32[]{:S(2)}) collective-permute-start(bf16[1,2,512,128]{3,2,1,0:T(8,128)(2,1)S(1)} %get-tuple-element.50), channel_id=1, source_target_pairs={{0,5},{1,6},{2,7},{3,0},{4,1},{5,2},{6,3},{7,4},{8,13},{9,14},{10,... | collective-permute-start | bytes 786440 | tf_op jit(solution)/shard_map/ppermute | solution.py:539
  82.1 81.7 %collective-permute-start.3 = (bf16[1,2,512,128]{3,2,1,0:T(8,128)(2,1)S(1)}, bf16[1,2,512,128]{3,2,1,0:T(8,128)(2,1)S(1)}, u32[]{:S(2)}, u32[]{:S(2)}) collective-permute-start(bf16[1,2,512,128]{3,2,1,0:T(8,128)(2,1)S(1)} %get-tuple-element.48), channel_id=1, source_target_pairs={{0,7},{1,0},{2,1},{3,2},{4,3},{5,4},{6,5},{7,6},{8,15},{9,8},{10,9... | collective-permute-start | bytes 786440 | tf_op jit(solution)/shard_map/ppermute | solution.py:539
  86.2 75.9 %collective-permute-start.2 = (bf16[1,2,512,128]{3,2,1,0:T(8,128)(2,1)S(1)}, bf16[1,2,512,128]{3,2,1,0:T(8,128)(2,1)}, u32[]{:S(2)}, u32[]{:S(2)}) collective-permute-start(bf16[1,2,512,128]{3,2,1,0:T(8,128)(2,1)S(1)} %get-tuple-element.49), channel_id=1, source_target_pairs={{0,6},{1,7},{2,0},{3,1},{4,2},{5,3},{6,4},{7,5},{8,14},{9,15},{10,... | collective-permute-start | bytes 786440 | tf_op jit(solution)/shard_map/ppermute | solution.py:539
  93.1 1.6 copy-start.2
  94.7 0.9 copy-start.8
  127.9 1.0 copy-start.5
  128.9 0.7 copy-start.7
  129.7 1.4 copy-start.9
  131.0 26.5 %copy-start.10 = (u32[32]{0:T(128)S(1)}, u32[32]{0:T(128)}, u32[]{:S(2)}) copy-start(u32[32]{0:T(128)} %constant.32) | copy-start | bytes 388
